TPU v7x, 256 devices: a whole 4x4x8 slice. The times are simulated.
256 devices in a mesh: gx: 16 (over z, core), yz: 16 (over y, x).
Axes of the slice: x: 4, y: 4, z: 8, core: 2. Of those that a mesh axis runs over, the one named last changes fastest.
Arguments:
- loads: float32 [16, 294912], P(None, ('gx', 'yz')), may hold values from -30 to 30
- stiffness: bfloat16 [294912, 1152], P(('gx', 'yz')), may hold values from -1 to 16, as said below
- local_inverse: bfloat16 [294912, 1152], P(('gx', 'yz')), may hold values from -1 to 2, as said below
- coarse_basis: bfloat16 [24, 294912], P(None, ('gx', 'yz')), may hold values from -0.1875 to 0.1875
- coarse_inverse: bfloat16 [1024, 1024], replicated, may hold values from -1 to 2, as said below
- primal_index: int32 [256, 24], P(('gx', 'yz')), may hold values from 0 to 1023, as said below
- layer_counts: int32 [256, 2], P(('gx', 'yz')), may hold values from 0 to 144, as said below
- layer_index: int32 [256, 2, 144], P(('gx', 'yz')), may hold values from 0 to 1151, as said below
- across_counts: int32 [256, 16], P(('gx', 'yz')), may hold values from 0 to 48, as said below
- across_index: int32 [256, 16, 48], P(('gx', 'yz')), may hold values from 0 to 1151, as said below
Outputs:
- solution: float32 [16, 294912], P(None, ('gx', 'yz'))
- residual: float32 [16, 294912], P(None, ('gx', 'yz'))
- precond: float32 [16, 294912], P(None, ('gx', 'yz'))
Inputs may be any that keep to these rules, and one draw needn't show every extreme that they name: `stiffness`: each subdomain's block of 1152 rows is symmetric positive definite. `local_inverse`: each subdomain's block of 1152 rows is symmetric positive definite. `coarse_inverse`: symmetric positive definite. `primal_index`: the 24 entries of one subdomain are distinct. layer_counts[s, 1] equals layer_counts[s + 16, 0]; the lower count is 0 on the first layer and the upper count 0 on the last; for one position p across, drawn afresh, every two adjacent layers share exactly 144 dofs there. `layer_index`: entry j of subdomain s's upper list and entry j of subdomain s + 16's lower list name the same shared dof; entries past a count are 0; all list entries of one subdomain, layer and across lists together, are distinct. across_counts[g * 16 + p, q] equals across_counts[g * 16 + q, p]; it is 0 for q = p, exactly 48 for q = p + 1 and q = p - 1 (mod 16), and in each layer one subdomain shares exactly 48 with every other one. `across_index`: entry j of subdomain s's list toward t and entry j of t's list toward s name the same shared dof; entries past a count are 0.
All inputs are finite; a program needn't handle non-finite values.
Results may differ from a plain program's by a relative error of at most 0.025.
Values may be sent and summed in bfloat16 or wider, within the bound.
A program may use at most 64 MiB of HBM per device.

v0:
```python
import jax
import jax.numpy as jnp
from jax import lax
from jax.sharding import PartitionSpec as P

ITERS = 2


def extended(value, sides, width):
    for axis, dim in sides:
        count, length = (lax.axis_size(axis), value.shape[dim])
        up = [(i, (i + 1) % count) for i in range(count - 1)]
        down = [(j, i) for i, j in up]
        last = lax.slice_in_dim(value, length - width, length, axis=dim)
        initial = lax.slice_in_dim(value, 0, width, axis=dim)
        before = lax.ppermute(last, axis, up)
        after = lax.ppermute(initial, axis, down)
        value = jnp.concatenate([before, value, after], axis=dim)
    return value


def inner_product(left, right):
    return lax.dot_general(
        left,
        right,
        (((1,), (1,)), ((), ())),
        precision=lax.Precision.HIGHEST,
        preferred_element_type=jnp.float32,
    )


def spd_solve(matrix, right_side):
    lower = jnp.linalg.cholesky(matrix)
    middle = lax.linalg.triangular_solve(lower, right_side, left_side=True, lower=True)
    return lax.linalg.triangular_solve(lower, middle, left_side=True, lower=True, transpose_a=True)


def assemble(vector, lists):
    layer_list, layer_mask, across_list, across_mask = lists
    cases = vector.shape[0]
    outgoing = jnp.take(vector, layer_list, axis=1) * layer_mask[None]
    framed = extended(outgoing, (("gx", 1),), 1)
    sending = jnp.take(vector, across_list, axis=1) * across_mask[None]
    arrived = lax.all_to_all(
        sending.astype(jnp.bfloat16), "yz", split_axis=1, concat_axis=1, tiled=True
    ).astype(sending.dtype)
    summed = vector.at[:, across_list.reshape(-1)].add(arrived.reshape(cases, -1))
    summed = summed.at[:, layer_list[0]].add(framed[:, 0])
    return summed.at[:, layer_list[1]].add(framed[:, 3])


def dof_weight(length, lists):
    layer_list, layer_mask, across_list, across_mask = lists
    shared = jnp.zeros((length,), jnp.float32)
    shared = shared.at[layer_list.reshape(-1)].add(layer_mask.reshape(-1))
    shared = shared.at[across_list.reshape(-1)].add(across_mask.reshape(-1))
    return 1.0 / (1.0 + shared)


def precondition(residual, weight, local_inverse, coarse_basis, coarse_inverse, primal, lists):
    weighted = (weight[None] * residual).astype(jnp.bfloat16)
    local_part = jnp.dot(weighted, local_inverse, preferred_element_type=jnp.float32)
    coarse_terms = lax.dot_general(
        weighted, coarse_basis, (((1,), (1,)), ((), ())), preferred_element_type=jnp.float32
    )
    coarse_size = coarse_inverse.shape[0]
    selector = (primal[:, None] == jnp.arange(coarse_size)[None, :]).astype(jnp.float32)
    spread = jnp.dot(coarse_terms, selector, precision=lax.Precision.HIGHEST)
    coarse_total = lax.psum(spread, ("gx", "yz"))
    coarse_rhs = coarse_total.astype(jnp.bfloat16)
    row_count = coarse_size // lax.axis_size("gx")
    row_block = lax.dynamic_slice_in_dim(
        coarse_inverse, lax.axis_index("gx") * row_count, row_count, 0
    )
    own_rows = lax.dot_general(
        coarse_rhs, row_block, (((1,), (1,)), ((), ())), preferred_element_type=jnp.float32
    ).astype(jnp.bfloat16)
    coarse_solution = lax.all_gather(own_rows, "gx", axis=1, tiled=True)
    picked = jnp.take(coarse_solution, primal, axis=1)
    coarse_part = jnp.dot(picked, coarse_basis, preferred_element_type=jnp.float32)
    assembled = assemble(weight[None] * (local_part + coarse_part), lists)
    gram = lax.psum(inner_product(weight[None] * assembled, residual), ("gx", "yz"))
    return (assembled, gram)


def per_device(
    loads,
    stiffness,
    local_inverse,
    coarse_basis,
    coarse_inverse,
    primal_index,
    layer_counts,
    layer_index,
    across_counts,
    across_index,
):
    layer_list = layer_index[0]
    across_list = across_index[0]
    layer_mask = (jnp.arange(layer_list.shape[1])[None, :] < layer_counts[0][:, None]).astype(
        jnp.float32
    )
    across_mask = (jnp.arange(across_list.shape[1])[None, :] < across_counts[0][:, None]).astype(
        jnp.float32
    )
    lists = (layer_list, layer_mask, across_list, across_mask)
    weight = dof_weight(loads.shape[1], lists)
    primal = primal_index[0]

    def apply_preconditioner(current):
        return precondition(
            current, weight, local_inverse, coarse_basis, coarse_inverse, primal, lists
        )

    residual = assemble(loads, lists)
    solution = jnp.zeros_like(residual)
    precond, product = apply_preconditioner(residual)
    direction = precond
    for iteration in range(ITERS):
        stiff_image = jnp.dot(
            direction.astype(jnp.bfloat16), stiffness, preferred_element_type=jnp.float32
        )
        curvature = lax.psum(inner_product(direction, stiff_image), ("gx", "yz"))
        image = assemble(stiff_image, lists)
        alpha = spd_solve(curvature, product)
        solution = solution + jnp.dot(alpha.T, direction, precision=lax.Precision.HIGHEST)
        residual = residual - jnp.dot(alpha.T, image, precision=lax.Precision.HIGHEST)
        precond, product_next = apply_preconditioner(residual)
        if iteration + 1 < ITERS:
            beta = spd_solve(product, product_next)
            direction = precond + jnp.dot(beta.T, direction, precision=lax.Precision.HIGHEST)
        product = product_next
    return (solution, residual, precond)


def solution(mesh):
    in_specs = (
        P(None, ("gx", "yz")),
        P(("gx", "yz"), None),
        P(("gx", "yz"), None),
        P(None, ("gx", "yz")),
        P(),
        P(("gx", "yz"), None),
        P(("gx", "yz"), None),
        P(("gx", "yz"), None, None),
        P(("gx", "yz"), None),
        P(("gx", "yz"), None, None),
    )
    out_specs = (P(None, ("gx", "yz")), P(None, ("gx", "yz")), P(None, ("gx", "yz")))
    return jax.shard_map(
        per_device, mesh=mesh, in_specs=in_specs, out_specs=out_specs, check_vma=False
    )
```

profile of v0, /device:TPU:1, one launch (start us, length us, event | category | flops | bytes accessed | tf_op | source)
XLA Modules:
  0.0 816.1 jit_solution(10036473766111364378)
XLA Ops:
  5.4 5.1 collective-permute-start.1
  18.3 6.5 all-to-all-start
  25.8 3.6 scatter_custom_fusion
  29.4 5.6 scatter_fusion
  35.5 7.8 scatter_fusion.1
  43.3 3.5 scatter_custom_fusion.3
  46.8 3.6 scatter_custom_fusion.4
  52.1 79.4 %psum.49 = bf16[16,1024]{1,0:T(8,128)(2,1)S(1)} all-reduce(f32[16,1024]{1,0:T(8,128)S(1)} %fusion.19), channel_id=1, replica_groups=mesh['gx'=16,'yz'=16] {'gx','yz'}, use_global_device_ids=true, to_apply=%region_5.8 | all-reduce | flops 16384 | bytes 98304 | tf_op jit(solution)/shard_map/psum | solution.py:69
  132.5 16.6 %all-gather = bf16[16,64,16]{1,2,0:T(8,128)(2,1)S(1)} all-gather(bf16[1,64,16]{1,2,0:T(8,128)(2,1)S(1)} %fusion.3), channel_id=1, replica_groups=mesh['gx'=16,'yz'=16] {'gx'}, dimensions={0}, use_global_device_ids=true | all-gather | bytes 34816 | tf_op jit(solution)/shard_map/all_gather | solution.py:78
  160.1 3.5 all-to-all-start.1
  167.1 3.0 collective-permute-start.3
  172.8 7.4 scatter_fusion.2
  188.8 2.8 gather_fusion.6
  191.6 3.3 gather_fusion.5
  197.0 76.2 %all-reduce = (f32[16,16]{0,1:T(8,128)S(1)}, f32[16,16]{0,1:T(8,128)S(1)}) all-reduce(f32[16,16]{0,1:T(8,128)S(1)} %fusion.46, f32[16,16]{0,1:T(8,128)} %fusion.117), channel_id=1, replica_groups=mesh['gx'=16,'yz'=16] {'gx','yz'}, use_global_device_ids=true, to_apply=%region_12.17 | all-reduce | flops 512 | bytes 4096 | tf_op jit(solution)/shard_map/psum | solution.py:82
  283.7 3.0 collective-permute-start.4
  290.2 3.5 all-to-all-start.2
  294.3 5.8 all-to-all-done.2
  302.8 8.2 %scatter_fusion.3 = f32[16,1152]{0,1:T(8,128)} fusion(f32[16,1152]{0,1:T(8,128)} %copy.143, s32[768]{0:T(1024)S(1)} %fusion.94, f32[768,16]{1,0:T(8,128)} %copy.144), kind=kCustom, calls=%fused_computation.23 | custom fusion | flops 12288 | bytes 150528 | tf_op jit(solution)/shard_map/scatter-add | solution.py:47
  311.0 3.5 scatter_custom_fusion.9
  314.5 3.8 scatter_custom_fusion.10
  321.5 73.8 %psum.52 = bf16[16,1024]{1,0:T(8,128)(2,1)} all-reduce(f32[16,1024]{1,0:T(8,128)S(1)} %fusion.18), channel_id=1, replica_groups=mesh['gx'=16,'yz'=16] {'gx','yz'}, use_global_device_ids=true, to_apply=%region_16.0 | all-reduce | flops 16384 | bytes 98304 | tf_op jit(solution)/shard_map/psum | solution.py:69
  396.4 17.0 %all-gather.1 = bf16[16,64,16]{1,2,0:T(8,128)(2,1)S(1)} all-gather(bf16[1,64,16]{1,2,0:T(8,128)(2,1)S(1)} %fusion.4), channel_id=1, replica_groups=mesh['gx'=16,'yz'=16] {'gx'}, dimensions={0}, use_global_device_ids=true | all-gather | bytes 34816 | tf_op jit(solution)/shard_map/all_gather | solution.py:78
  421.3 3.3 gather_fusion.8
  428.4 3.5 collective-permute-start.6
  435.4 3.5 all-to-all-start.3
  441.4 4.1 all-to-all-done.3
  448.3 8.2 %scatter_fusion.4 = f32[16,1152]{0,1:T(8,128)} fusion(f32[16,1152]{0,1:T(8,128)} %copy.152, s32[768]{0:T(1024)S(1)} %fusion.94, f32[768,16]{1,0:T(8,128)} %copy.153), kind=kCustom, calls=%fused_computation.26 | custom fusion | flops 12288 | bytes 150528 | tf_op jit(solution)/shard_map/scatter-add | solution.py:47
  456.5 3.5 scatter_custom_fusion.12
  460.0 3.6 scatter_custom_fusion.13
  465.1 72.7 %psum.53 = f32[16,16]{1,0:T(8,128)S(1)} all-reduce(f32[16,16]{1,0:T(8,128)S(1)} %fusion.44), channel_id=1, replica_groups=mesh['gx'=16,'yz'=16] {'gx','yz'}, use_global_device_ids=true, to_apply=%region_20.27 | all-reduce | flops 256 | bytes 2048 | tf_op jit(solution)/shard_map/psum | solution.py:82
  546.1 3.3 gather_fusion.10
  549.4 73.5 %psum.54 = f32[16,16]{0,1:T(8,128)S(1)} all-reduce(f32[16,16]{0,1:T(8,128)} %fusion.118), channel_id=1, replica_groups=mesh['gx'=16,'yz'=16] {'gx','yz'}, use_global_device_ids=true, to_apply=%region_21.28 | all-reduce | flops 256 | bytes 2048 | tf_op jit(solution)/shard_map/psum | solution.py:123
  633.0 3.4 collective-permute-start.8
  639.8 4.4 all-to-all-start.4
  645.2 5.7 all-to-all-done.4
  654.3 8.2 %scatter_fusion.5 = f32[16,1152]{0,1:T(8,128)} fusion(f32[16,1152]{0,1:T(8,128)} %copy.163, s32[768]{0:T(1024)S(1)} %fusion.94, f32[768,16]{1,0:T(8,128)} %copy.164), kind=kCustom, calls=%fused_computation.29 | custom fusion | flops 12288 | bytes 150528 | tf_op jit(solution)/shard_map/scatter-add | solution.py:47
  662.5 3.5 scatter_custom_fusion.15
  666.0 3.6 scatter_custom_fusion.16
  673.5 73.6 %psum.55 = bf16[16,1024]{1,0:T(8,128)(2,1)} all-reduce(f32[16,1024]{1,0:T(8,128)} %fusion.17), channel_id=1, replica_groups=mesh['gx'=16,'yz'=16] {'gx','yz'}, use_global_device_ids=true, to_apply=%region_25.32 | all-reduce | flops 16384 | bytes 98304 | tf_op jit(solution)/shard_map/psum | solution.py:69
  748.2 17.6 %all-gather.2 = bf16[16,64,16]{1,2,0:T(8,128)(2,1)} all-gather(bf16[1,64,16]{1,2,0:T(8,128)(2,1)S(1)} %fusion.5), channel_id=1, replica_groups=mesh['gx'=16,'yz'=16] {'gx'}, dimensions={0}, use_global_device_ids=true | all-gather | bytes 34816 | tf_op jit(solution)/shard_map/all_gather | solution.py:78
  776.0 3.3 gather_fusion.13
  783.1 3.5 collective-permute-start.10
  788.6 3.7 all-to-all-start.5
  794.2 4.4 all-to-all-done.5
  799.1 7.8 scatter_fusion.6
  806.9 3.5 scatter_custom_fusion.18
  810.4 3.6 scatter_custom_fusion.19
  (205 shorter events, 139.0 us)
Async XLA Ops:
  0.6 148.5 %copy-start = (bf16[1152,1152]{1,0:T(8,128)(2,1)S(1)}, bf16[1152,1152]{1,0:T(8,128)(2,1)}, u32[]{:S(2)}) copy-start(bf16[1152,1152]{1,0:T(8,128)(2,1)} %param.23) | copy-start | bytes 7962628
  0.6 24.7 %copy-start.10 = (s32[1,2,144]{2,1,0:T(2,128)S(1)}, s32[1,2,144]{2,1,0:T(2,128)}, u32[]{:S(2)}) copy-start(s32[1,2,144]{2,1,0:T(2,128)} %param.28) | copy-start | bytes 3460
  0.7 24.8 %copy-start.6 = (s32[1,16,48]{2,1,0:T(8,128)S(1)}, s32[1,16,48]{2,1,0:T(8,128)}, u32[]{:S(2)}) copy-start(s32[1,16,48]{2,1,0:T(8,128)} %param.30) | copy-start | bytes 9220
  0.7 24.1 %copy-start.12 = (s32[1,24]{1,0:T(1,128)S(1)}, s32[1,24]{1,0:T(1,128)}, u32[]{:S(2)}) copy-start(s32[1,24]{1,0:T(1,128)} %param.26) | copy-start | bytes 292
  1.6 11.6 %copy-start.7 = (s32[1024]{0:T(1024)}, s32[1024]{0:T(1024)S(1)}, u32[]{:S(2)}) copy-start(s32[1024]{0:T(1024)S(1)} %pad_clamp_fusion.1) | copy-start | bytes 12292
  2.4 10.9 %copy-start.8 = (pred[2,144]{1,0:T(4,128)(4,1)}, pred[2,144]{1,0:T(4,128)(4,1)S(1)}, u32[]{:S(2)}) copy-start(pred[2,144]{1,0:T(4,128)(4,1)S(1)} %get-tuple-element.39) | copy-start | bytes 868
  3.5 22.2 %copy-start.1 = (f32[16,1152]{0,1:T(8,128)}, f32[16,1152]{0,1:T(8,128)S(1)}, u32[]{:S(2)}) copy-start(f32[16,1152]{0,1:T(8,128)S(1)} %copy.124) | copy-start | bytes 221188
  5.4 41.4 %collective-permute-start.1 = (f32[16,1,144]{0,2,1:T(8,128)}, f32[16,1,144]{0,2,1:T(8,128)}, u32[]{:S(2)}, u32[]{:S(2)}) collective-permute-start(f32[16,1,144]{0,2,1:T(8,128)} %get-tuple-element.33), channel_id=1, source_target_pairs={{16,0},{32,16},{48,32},{64,48},{80,64},{96,80},{112,96},{128,112},... | collective-permute-start | bytes 27656 | tf_op jit(solution)/shard_map/ppermute | solution.py:17
  10.5 32.8 %collective-permute-start = (f32[16,1,144]{0,2,1:T(8,128)}, f32[16,1,144]{0,2,1:T(8,128)}, u32[]{:S(2)}, u32[]{:S(2)}) collective-permute-start(f32[16,1,144]{0,2,1:T(8,128)} %get-tuple-element.34), channel_id=1, source_target_pairs={{0,16},{16,32},{32,48},{48,64},{64,80},{80,96},{96,112},{112,128},... | collective-permute-start | bytes 27656 | tf_op jit(solution)/shard_map/ppermute | solution.py:16
  18.3 16.8 %all-to-all-start = ((bf16[16,2,384]{2,1,0:T(2,128)(2,1)}), bf16[16,2,384]{2,1,0:T(2,128)(2,1)S(1)}, u32[]{:S(2)}, u32[]{:S(2)}) async-start(bf16[16,2,384]{2,1,0:T(2,128)(2,1)} %reshape.687), calls=%async_computation | async-start | bytes 49152 | tf_op jit(solution)/shard_map/all_to_all | solution.py:44
  25.5 17.8 %copy-start.16 = (s32[144,1]{0,1:T(1,128)}, s32[144,1]{0,1:T(1,128)S(1)}, u32[]{:S(2)}) copy-start(s32[144,1]{0,1:T(1,128)S(1)} %get-tuple-element.36) | copy-start | bytes 1732
  25.5 21.3 %copy-start.15 = (s32[144,1]{0,1:T(1,128)}, s32[144,1]{0,1:T(1,128)S(1)}, u32[]{:S(2)}) copy-start(s32[144,1]{0,1:T(1,128)S(1)} %get-tuple-element.35) | copy-start | bytes 1732
  35.0 16.7 %copy-start.2 = (bf16[24,1152]{1,0:T(8,128)(2,1)S(1)}, bf16[24,1152]{1,0:T(8,128)(2,1)}, u32[]{:S(2)}) copy-start(bf16[24,1152]{1,0:T(8,128)(2,1)} %param.24) | copy-start | bytes 165892
  35.0 16.8 %copy-start.13 = (s32[1,24]{1,0:T(1,128)S(1)}, s32[1,24]{1,0:T(1,128)}, u32[]{:S(2)}) copy-start(s32[1,24]{1,0:T(1,128)} %param.26) | copy-start | bytes 292
  35.0 114.7 %copy-start.11 = (s32[1024]{0:T(1024)}, s32[1024]{0:T(1024)S(1)}, u32[]{:S(2)}) copy-start(s32[1024]{0:T(1024)S(1)} %pad_clamp_fusion) | copy-start | bytes 12292
  46.8 103.6 %copy-start.14 = (pred[24]{0:T(512)(128)(4,1)S(1)}, pred[24]{0:T(512)(128)(4,1)}, u32[]{:S(2)}) copy-start(pred[24]{0:T(512)(128)(4,1)} %compare_and_fusion.2) | copy-start | bytes 76
  160.1 10.0 %all-to-all-start.1 = ((bf16[16,2,384]{2,1,0:T(2,128)(2,1)}), bf16[16,2,384]{2,1,0:T(2,128)(2,1)S(1)}, u32[]{:S(2)}, u32[]{:S(2)}) async-start(bf16[16,2,384]{2,1,0:T(2,128)(2,1)} %reshape.689), calls=%async_computation.1 | async-start | bytes 49152 | tf_op jit(solution)/shard_map/all_to_all | solution.py:44
  165.2 15.1 %collective-permute-start.2 = (f32[16,1,144]{0,2,1:T(8,128)}, f32[16,1,144]{0,2,1:T(8,128)}, u32[]{:S(2)}, u32[]{:S(2)}) collective-permute-start(f32[16,1,144]{0,2,1:T(8,128)} %get-tuple-element.32), channel_id=1, source_target_pairs={{0,16},{16,32},{32,48},{48,64},{64,80},{80,96},{96,112},{112,128},... | collective-permute-start | bytes 27656 | tf_op jit(solution)/shard_map/ppermute | solution.py:16
  167.1 15.1 %collective-permute-start.3 = (f32[16,1,144]{0,2,1:T(8,128)}, f32[16,1,144]{0,2,1:T(8,128)}, u32[]{:S(2)}, u32[]{:S(2)}) collective-permute-start(f32[16,1,144]{0,2,1:T(8,128)} %get-tuple-element.31), channel_id=1, source_target_pairs={{16,0},{32,16},{48,32},{64,48},{80,64},{96,80},{112,96},{128,112},... | collective-permute-start | bytes 27656 | tf_op jit(solution)/shard_map/ppermute | solution.py:17
  277.8 42.2 %copy-start.4 = (f32[16,16]{1,0:T(8,128)}, f32[16,16]{1,0:T(8,128)S(1)}, u32[]{:S(2)}) copy-start(f32[16,16]{1,0:T(8,128)S(1)} %fusion.79) | copy-start | bytes 3076
  279.2 11.0 %copy-start.9 = (f32[16,16]{1,0:T(8,128)}, f32[16,16]{1,0:T(8,128)S(1)}, u32[]{:S(2)}) copy-start(f32[16,16]{1,0:T(8,128)S(1)} %cholesky.70) | copy-start | bytes 3076
  281.0 33.5 %collective-permute-start.5 = (f32[16,1,144]{0,2,1:T(8,128)}, f32[16,1,144]{0,2,1:T(8,128)}, u32[]{:S(2)}, u32[]{:S(2)}) collective-permute-start(f32[16,1,144]{0,2,1:T(8,128)} %get-tuple-element.29), channel_id=1, source_target_pairs={{16,0},{32,16},{48,32},{64,48},{80,64},{96,80},{112,96},{128,112},... | collective-permute-start | bytes 27656 | tf_op jit(solution)/shard_map/ppermute | solution.py:17
  283.7 27.3 %collective-permute-start.4 = (f32[16,1,144]{0,2,1:T(8,128)}, f32[16,1,144]{0,2,1:T(8,128)}, u32[]{:S(2)}, u32[]{:S(2)}) collective-permute-start(f32[16,1,144]{0,2,1:T(8,128)} %get-tuple-element.30), channel_id=1, source_target_pairs={{0,16},{16,32},{32,48},{48,64},{64,80},{80,96},{96,112},{112,128},... | collective-permute-start | bytes 27656 | tf_op jit(solution)/shard_map/ppermute | solution.py:16
  290.2 9.9 %all-to-all-start.2 = ((bf16[16,2,384]{2,1,0:T(2,128)(2,1)}), bf16[16,2,384]{2,1,0:T(2,128)(2,1)S(1)}, u32[]{:S(2)}, u32[]{:S(2)}) async-start(bf16[16,2,384]{2,1,0:T(2,128)(2,1)} %reshape.691), calls=%async_computation.2 | async-start | bytes 49152 | tf_op jit(solution)/shard_map/all_to_all | solution.py:44
  426.4 33.6 %collective-permute-start.7 = (f32[16,1,144]{0,2,1:T(8,128)}, f32[16,1,144]{0,2,1:T(8,128)}, u32[]{:S(2)}, u32[]{:S(2)}) collective-permute-start(f32[16,1,144]{0,2,1:T(8,128)} %get-tuple-element.27), channel_id=1, source_target_pairs={{16,0},{32,16},{48,32},{64,48},{80,64},{96,80},{112,96},{128,112},... | collective-permute-start | bytes 27656 | tf_op jit(solution)/shard_map/ppermute | solution.py:17
  428.4 28.0 %collective-permute-start.6 = (f32[16,1,144]{0,2,1:T(8,128)}, f32[16,1,144]{0,2,1:T(8,128)}, u32[]{:S(2)}, u32[]{:S(2)}) collective-permute-start(f32[16,1,144]{0,2,1:T(8,128)} %get-tuple-element.28), channel_id=1, source_target_pairs={{0,16},{16,32},{32,48},{48,64},{64,80},{80,96},{96,112},{112,128},... | collective-permute-start | bytes 27656 | tf_op jit(solution)/shard_map/ppermute | solution.py:16
  435.4 10.1 %all-to-all-start.3 = ((bf16[16,2,384]{2,1,0:T(2,128)(2,1)}), bf16[16,2,384]{2,1,0:T(2,128)(2,1)S(1)}, u32[]{:S(2)}, u32[]{:S(2)}) async-start(bf16[16,2,384]{2,1,0:T(2,128)(2,1)} %reshape.693), calls=%async_computation.3 | async-start | bytes 49152 | tf_op jit(solution)/shard_map/all_to_all | solution.py:44
  537.8 0.6 copy-start.5
  630.4 35.6 %collective-permute-start.9 = (f32[16,1,144]{0,2,1:T(8,128)}, f32[16,1,144]{0,2,1:T(8,128)}, u32[]{:S(2)}, u32[]{:S(2)}) collective-permute-start(f32[16,1,144]{0,2,1:T(8,128)} %get-tuple-element.25), channel_id=1, source_target_pairs={{16,0},{32,16},{48,32},{64,48},{80,64},{96,80},{112,96},{128,112},... | collective-permute-start | bytes 27656 | tf_op jit(solution)/shard_map/ppermute | solution.py:17
  633.0 29.5 %collective-permute-start.8 = (f32[16,1,144]{0,2,1:T(8,128)}, f32[16,1,144]{0,2,1:T(8,128)}, u32[]{:S(2)}, u32[]{:S(2)}) collective-permute-start(f32[16,1,144]{0,2,1:T(8,128)} %get-tuple-element.26), channel_id=1, source_target_pairs={{0,16},{16,32},{32,48},{48,64},{64,80},{80,96},{96,112},{112,128},... | collective-permute-start | bytes 27656 | tf_op jit(solution)/shard_map/ppermute | solution.py:16
  639.8 11.0 %all-to-all-start.4 = ((bf16[16,2,384]{2,1,0:T(2,128)(2,1)}), bf16[16,2,384]{2,1,0:T(2,128)(2,1)}, u32[]{:S(2)}, u32[]{:S(2)}) async-start(bf16[16,2,384]{2,1,0:T(2,128)(2,1)} %reshape.695), calls=%async_computation.4 | async-start | bytes 49152 | tf_op jit(solution)/shard_map/all_to_all | solution.py:44
  671.3 108.0 %copy-start.3 = (f32[16,1152]{1,0:T(8,128)}, f32[16,1152]{1,0:T(8,128)S(1)}, u32[]{:S(2)}) copy-start(f32[16,1152]{1,0:T(8,128)S(1)} %convolution_subtract_fusion) | copy-start | bytes 221188
  781.1 29.3 %collective-permute-start.11 = (f32[16,1,144]{0,2,1:T(8,128)}, f32[16,1,144]{0,2,1:T(8,128)}, u32[]{:S(2)}, u32[]{:S(2)}) collective-permute-start(f32[16,1,144]{0,2,1:T(8,128)} %get-tuple-element.23), channel_id=1, source_target_pairs={{16,0},{32,16},{48,32},{64,48},{80,64},{96,80},{112,96},{128,112},... | collective-permute-start | bytes 27656 | tf_op jit(solution)/shard_map/ppermute | solution.py:17
  783.1 23.8 %collective-permute-start.10 = (f32[16,1,144]{0,2,1:T(8,128)}, f32[16,1,144]{0,2,1:T(8,128)}, u32[]{:S(2)}, u32[]{:S(2)}) collective-permute-start(f32[16,1,144]{0,2,1:T(8,128)} %get-tuple-element.24), channel_id=1, source_target_pairs={{0,16},{16,32},{32,48},{48,64},{64,80},{80,96},{96,112},{112,128},... | collective-permute-start | bytes 27656 | tf_op jit(solution)/shard_map/ppermute | solution.py:16
  788.6 10.1 %all-to-all-start.5 = ((bf16[16,2,384]{2,1,0:T(2,128)(2,1)}), bf16[16,2,384]{2,1,0:T(2,128)(2,1)S(1)}, u32[]{:S(2)}, u32[]{:S(2)}) async-start(bf16[16,2,384]{2,1,0:T(2,128)(2,1)} %reshape.697), calls=%async_computation.5 | async-start | bytes 49152 | tf_op jit(solution)/shard_map/all_to_all | solution.py:44
where the time goes:
time: 829 us; the launch traced here: 816 us
  blocking collectives  500 us (60%)
  other arithmetic  123 us (15%)
  local copies, waits for them, and re-layouts  83 us (10%)
  starting transfers between devices  59.8 us (7%)
  matrix products  28.6 us (3%)
  waiting for transfers between devices  20.1 us (2%)
    psum x3, blocking collectives, precondition(): coarse_total = lax.psum(spread, ('gx', 'yz'))  227 us
    psum x2, blocking collectives, precondition(): lax.psum(inner_product(weight[None] * assembled, residual), ('gx', 'yz'))  149 us
    psum x1, blocking collectives, per_device(): curvature = lax.psum(inner_product(direction, stiff_image), ('gx', 'yz'))  73.5 us
    all_gather x3, blocking collectives, precondition(): coarse_solution = lax.all_gather(own_rows, 'gx', axis=1, tiled=True)  51.2 us
    scatter-add x6, other arithmetic, assemble(): vector.at[:, across_list.reshape(-1)].add(arrived.reshape(cases, -1))  47.6 us
    gather x12, local copies, waits for them, and re-layouts, assemble(): sending = jnp.take(vector, across_list, axis=1) * across_mask[None]  27.3 us
    all_to_all x6, starting transfers between devices, assemble(): lax.all_to_all(sending.astype(jnp.bfloat16), 'yz', split_axis=1, concat_a...  25.1 us
    scatter-add x6, other arithmetic, assemble(): return summed.at[:, layer_list[1]].add(framed[:, 3])  20.3 us
  transfers between devices with their start and end apart: 18, of which 4 were waited for; matrix products, arithmetic and copies ran while one was open for 14% of the time, Pallas kernels for 0%

commit v1 on v0

--- a/solution.py
+++ b/solution.py
@@ -4,6 +4,11 @@
 from jax.sharding import PartitionSpec as P
 
 ITERS = 2
+
+
+def summed_here(x, name):
+    parts = lax.all_gather(x, name)
+    return jnp.sum(parts, axis=0)
 
 
 def extended(value, sides, width):
@@ -79,7 +84,7 @@
     picked = jnp.take(coarse_solution, primal, axis=1)
     coarse_part = jnp.dot(picked, coarse_basis, preferred_element_type=jnp.float32)
     assembled = assemble(weight[None] * (local_part + coarse_part), lists)
-    gram = lax.psum(inner_product(weight[None] * assembled, residual), ("gx", "yz"))
+    gram = summed_here(inner_product(weight[None] * assembled, residual), ("gx", "yz"))
     return (assembled, gram)
 
 

time: 829 us -> 999 us (1.21)
  blocking collectives: 500 us -> 693 us
  waiting for transfers between devices: 20.1 us -> 0.05 us
    all_gather x0 -> x2, blocking collectives: none -> 254 us  [summed_here(): parts = lax.all_gather(x, name)]
    psum x2 -> x0, blocking collectives: 149 us -> none  [precondition(): lax.psum(inner_product(weight[None] * assembled, residual), ('gx', 'yz'))]
    psum x1 -> x2, blocking collectives: 73.5 us -> 161 us  [per_device(): curvature = lax.psum(inner_product(direction, stiff_image), ('gx', 'yz'))]
    all_to_all x6, waiting for transfers between devices: 20 us -> 0.02 us  [assemble(): lax.all_to_all(sending.astype(jnp.bfloat16), 'yz', split_axis=1, concat_a...]
  transfers between devices with their start and end apart: 18 -> 18, of which waited for: 4 -> 0; matrix products, arithmetic and copies ran while one was open for 14% -> 12% of each run, Pallas kernels for 0% -> 0%
where the time goes in v1:
time: 999 us; the launch traced here: 986 us
  blocking collectives  693 us (69%)
  other arithmetic  125 us (13%)
  local copies, waits for them, and re-layouts  82.5 us (8%)
  starting transfers between devices  57.9 us (6%)
  matrix products  26.6 us (3%)
    all_gather x2, blocking collectives, summed_here(): parts = lax.all_gather(x, name)  254 us
    psum x3, blocking collectives, precondition(): coarse_total = lax.psum(spread, ('gx', 'yz'))  226 us
    psum x2, blocking collectives, per_device(): curvature = lax.psum(inner_product(direction, stiff_image), ('gx', 'yz'))  161 us
    all_gather x3, blocking collectives, precondition(): coarse_solution = lax.all_gather(own_rows, 'gx', axis=1, tiled=True)  51.6 us
    scatter-add x6, other arithmetic, assemble(): vector.at[:, across_list.reshape(-1)].add(arrived.reshape(cases, -1))  47.2 us
    gather x12, local copies, waits for them, and re-layouts, assemble(): sending = jnp.take(vector, across_list, axis=1) * across_mask[None]  27.3 us
    all_to_all x6, starting transfers between devices, assemble(): lax.all_to_all(sending.astype(jnp.bfloat16), 'yz', split_axis=1, concat_a...  26 us
    scatter-add x6, other arithmetic, assemble(): return summed.at[:, layer_list[1]].add(framed[:, 3])  20.1 us
  transfers between devices with their start and end apart: 18, of which 0 were waited for; matrix products, arithmetic and copies ran while one was open for 12% of the time, Pallas kernels for 0%

profile of v1, /device:TPU:1, one launch (start us, length us, event | category | flops | bytes accessed | tf_op | source)
XLA Modules:
  0.0 986.0 jit_solution(12008260489394033336)
XLA Ops:
  7.7 7.6 all-to-all-start
  17.4 4.4 collective-permute-start
  24.7 3.6 scatter_custom_fusion
  28.3 5.6 scatter_fusion
  34.4 7.8 scatter_fusion.1
  42.2 3.5 scatter_custom_fusion.3
  45.7 3.6 scatter_custom_fusion.4
  50.9 80.0 %psum.35 = bf16[16,1024]{1,0:T(8,128)(2,1)S(1)} all-reduce(f32[16,1024]{1,0:T(8,128)S(1)} %fusion.19), channel_id=1, replica_groups=mesh['gx'=16,'yz'=16] {'gx','yz'}, use_global_device_ids=true, to_apply=%region_5.8 | all-reduce | flops 16384 | bytes 98304 | tf_op jit(solution)/shard_map/psum | solution.py:74
  132.0 15.9 %all-gather.2 = bf16[16,64,16]{1,2,0:T(8,128)(2,1)S(1)} all-gather(bf16[1,64,16]{1,2,0:T(8,128)(2,1)S(1)} %fusion.3), channel_id=1, replica_groups=mesh['gx'=16,'yz'=16] {'gx'}, dimensions={0}, use_global_device_ids=true | all-gather | bytes 34816 | tf_op jit(solution)/shard_map/all_gather | solution.py:83
  157.1 3.5 all-to-all-start.1
  162.3 2.6 collective-permute-start.2
  169.9 7.1 scatter_fusion.2
  184.6 3.3 gather_fusion.5
  187.9 2.8 gather_fusion.6
  193.3 127.2 %all-gather = f32[4096,16]{1,0:T(8,128)} all-gather(f32[16,16]{1,0:T(8,128)S(1)} %fusion.46), channel_id=2, replica_groups=mesh['gx'=16,'yz'=16] {'gx','yz'}, dimensions={0}, use_global_device_ids=true | all-gather | bytes 263168 | tf_op jit(solution)/shard_map/all_gather | solution.py:10
  327.3 3.8 all-to-all-start.2
  334.8 3.7 collective-permute-start.5
  338.4 80.4 %psum.36 = f32[16,16]{0,1:T(8,128)S(1)} all-reduce(f32[16,16]{0,1:T(8,128)S(1)} %copy-done.11), channel_id=1, replica_groups=mesh['gx'=16,'yz'=16] {'gx','yz'}, use_global_device_ids=true, to_apply=%region_9.13 | all-reduce | flops 256 | bytes 2048 | tf_op jit(solution)/shard_map/psum | solution.py:128
  426.8 8.2 scatter_fusion.3
  435.0 3.5 scatter_custom_fusion.9
  438.5 3.6 scatter_custom_fusion.10
  445.3 73.2 %psum.37 = bf16[16,1024]{1,0:T(8,128)(2,1)} all-reduce(f32[16,1024]{1,0:T(8,128)S(1)} %fusion.18), channel_id=1, replica_groups=mesh['gx'=16,'yz'=16] {'gx','yz'}, use_global_device_ids=true, to_apply=%region_16.0 | all-reduce | flops 16384 | bytes 98304 | tf_op jit(solution)/shard_map/psum | solution.py:74
  519.6 17.0 %all-gather.3 = bf16[16,64,16]{1,2,0:T(8,128)(2,1)S(1)} all-gather(bf16[1,64,16]{1,2,0:T(8,128)(2,1)S(1)} %fusion.4), channel_id=1, replica_groups=mesh['gx'=16,'yz'=16] {'gx'}, dimensions={0}, use_global_device_ids=true | all-gather | bytes 34816 | tf_op jit(solution)/shard_map/all_gather | solution.py:83
  541.7 3.3 gather_fusion.8
  545.1 2.8 gather_fusion.9
  551.3 3.5 all-to-all-start.3
  556.6 2.8 collective-permute-start.6
  566.8 8.2 scatter_fusion.4
  575.0 3.9 scatter_custom_fusion.12
  578.9 3.6 scatter_custom_fusion.13
  584.0 127.3 %all-gather.1 = f32[4096,16]{1,0:T(8,128)} all-gather(f32[16,16]{1,0:T(8,128)S(1)} %fusion.44), channel_id=3, replica_groups=mesh['gx'=16,'yz'=16] {'gx','yz'}, dimensions={0}, use_global_device_ids=true | all-gather | bytes 263168 | tf_op jit(solution)/shard_map/all_gather | solution.py:10
  717.8 3.3 gather_fusion.10
  721.1 2.8 gather_fusion.11
  728.2 4.1 all-to-all-start.4
  736.0 3.3 collective-permute-start.9
  739.3 80.2 %psum.38 = f32[16,16]{0,1:T(8,128)S(1)} all-reduce(f32[16,16]{0,1:T(8,128)} %fusion.118), channel_id=1, replica_groups=mesh['gx'=16,'yz'=16] {'gx','yz'}, use_global_device_ids=true, to_apply=%region_21.28 | all-reduce | flops 256 | bytes 2048 | tf_op jit(solution)/shard_map/psum | solution.py:128
  829.0 8.2 scatter_fusion.5
  837.2 3.5 scatter_custom_fusion.15
  840.7 3.6 scatter_custom_fusion.16
  848.1 73.1 %psum.39 = bf16[16,1024]{1,0:T(8,128)(2,1)} all-reduce(f32[16,1024]{1,0:T(8,128)} %fusion.17), channel_id=1, replica_groups=mesh['gx'=16,'yz'=16] {'gx','yz'}, use_global_device_ids=true, to_apply=%region_25.32 | all-reduce | flops 16384 | bytes 98304 | tf_op jit(solution)/shard_map/psum | solution.py:74
  922.3 18.7 %all-gather.4 = bf16[16,64,16]{1,2,0:T(8,128)(2,1)} all-gather(bf16[1,64,16]{1,2,0:T(8,128)(2,1)S(1)} %fusion.5), channel_id=1, replica_groups=mesh['gx'=16,'yz'=16] {'gx'}, dimensions={0}, use_global_device_ids=true | all-gather | bytes 34816 | tf_op jit(solution)/shard_map/all_gather | solution.py:83
  948.4 3.3 gather_fusion.13
  951.8 2.8 gather_fusion.14
  956.5 3.5 all-to-all-start.5
  961.7 2.8 collective-permute-start.10
  969.0 7.8 scatter_fusion.6
  976.8 3.5 scatter_custom_fusion.18
  980.3 3.6 scatter_custom_fusion.19
  (216 shorter events, 129.3 us)
Async XLA Ops:
  0.6 147.4 %copy-start = (bf16[1152,1152]{1,0:T(8,128)(2,1)S(1)}, bf16[1152,1152]{1,0:T(8,128)(2,1)}, u32[]{:S(2)}) copy-start(bf16[1152,1152]{1,0:T(8,128)(2,1)} %param.23) | copy-start | bytes 7962628
  0.6 23.1 %copy-start.7 = (s32[1,16,48]{2,1,0:T(8,128)S(1)}, s32[1,16,48]{2,1,0:T(8,128)}, u32[]{:S(2)}) copy-start(s32[1,16,48]{2,1,0:T(8,128)} %param.30) | copy-start | bytes 9220
  0.7 14.7 %copy-start.13 = (s32[1,2,144]{2,1,0:T(2,128)S(1)}, s32[1,2,144]{2,1,0:T(2,128)}, u32[]{:S(2)}) copy-start(s32[1,2,144]{2,1,0:T(2,128)} %param.28) | copy-start | bytes 3460
  0.7 15.8 %copy-start.20 = (s32[1,2]{1,0:T(1,128)S(1)}, s32[1,2]{1,0:T(1,128)}, u32[]{:S(2)}) copy-start(s32[1,2]{1,0:T(1,128)} %param.27) | copy-start | bytes 28
  0.7 23.4 %copy-start.15 = (s32[1,24]{1,0:T(1,128)S(1)}, s32[1,24]{1,0:T(1,128)}, u32[]{:S(2)}) copy-start(s32[1,24]{1,0:T(1,128)} %param.26) | copy-start | bytes 292
  2.8 21.9 %copy-start.1 = (f32[16,1152]{0,1:T(8,128)}, f32[16,1152]{0,1:T(8,128)S(1)}, u32[]{:S(2)}) copy-start(f32[16,1152]{0,1:T(8,128)S(1)} %copy.121) | copy-start | bytes 221188
  7.7 26.2 %all-to-all-start = ((bf16[16,2,384]{2,1,0:T(2,128)(2,1)}), bf16[16,2,384]{2,1,0:T(2,128)(2,1)S(1)}, u32[]{:S(2)}, u32[]{:S(2)}) async-start(bf16[16,2,384]{2,1,0:T(2,128)(2,1)} %reshape.689), calls=%async_computation | async-start | bytes 49152 | tf_op jit(solution)/shard_map/all_to_all | solution.py:49
  15.4 8.7 copy-start.8
  16.6 17.3 %copy-start.9 = (pred[2,144]{1,0:T(4,128)(4,1)}, pred[2,144]{1,0:T(4,128)(4,1)S(1)}, u32[]{:S(2)}) copy-start(pred[2,144]{1,0:T(4,128)(4,1)S(1)} %get-tuple-element.37) | copy-start | bytes 868
  17.4 24.8 %collective-permute-start = (f32[16,1,144]{0,2,1:T(8,128)}, f32[16,1,144]{0,2,1:T(8,128)}, u32[]{:S(2)}, u32[]{:S(2)}) collective-permute-start(f32[16,1,144]{0,2,1:T(8,128)} %get-tuple-element.32), channel_id=1, source_target_pairs={{0,16},{16,32},{32,48},{48,64},{64,80},{80,96},{96,112},{112,128},... | collective-permute-start | bytes 27656 | tf_op jit(solution)/shard_map/ppermute | solution.py:21
  21.8 23.9 %collective-permute-start.1 = (f32[16,1,144]{0,2,1:T(8,128)}, f32[16,1,144]{0,2,1:T(8,128)}, u32[]{:S(2)}, u32[]{:S(2)}) collective-permute-start(f32[16,1,144]{0,2,1:T(8,128)} %get-tuple-element.31), channel_id=1, source_target_pairs={{16,0},{32,16},{48,32},{64,48},{80,64},{96,80},{112,96},{128,112},... | collective-permute-start | bytes 27656 | tf_op jit(solution)/shard_map/ppermute | solution.py:22
  23.8 18.4 %copy-start.19 = (s32[144,1]{0,1:T(1,128)}, s32[144,1]{0,1:T(1,128)S(1)}, u32[]{:S(2)}) copy-start(s32[144,1]{0,1:T(1,128)S(1)} %get-tuple-element.34) | copy-start | bytes 1732
  23.8 21.8 %copy-start.18 = (s32[144,1]{0,1:T(1,128)}, s32[144,1]{0,1:T(1,128)S(1)}, u32[]{:S(2)}) copy-start(s32[144,1]{0,1:T(1,128)S(1)} %get-tuple-element.33) | copy-start | bytes 1732
  33.9 16.6 %copy-start.2 = (bf16[24,1152]{1,0:T(8,128)(2,1)S(1)}, bf16[24,1152]{1,0:T(8,128)(2,1)}, u32[]{:S(2)}) copy-start(bf16[24,1152]{1,0:T(8,128)(2,1)} %param.24) | copy-start | bytes 165892
  33.9 16.8 %copy-start.16 = (s32[1,24]{1,0:T(1,128)S(1)}, s32[1,24]{1,0:T(1,128)}, u32[]{:S(2)}) copy-start(s32[1,24]{1,0:T(1,128)} %param.26) | copy-start | bytes 292
  34.0 114.5 %copy-start.14 = (s32[1024]{0:T(1024)}, s32[1024]{0:T(1024)S(1)}, u32[]{:S(2)}) copy-start(s32[1024]{0:T(1024)S(1)} %pad_clamp_fusion) | copy-start | bytes 12292
  45.7 103.4 %copy-start.17 = (pred[24]{0:T(512)(128)(4,1)S(1)}, pred[24]{0:T(512)(128)(4,1)}, u32[]{:S(2)}) copy-start(pred[24]{0:T(512)(128)(4,1)} %compare_and_fusion.2) | copy-start | bytes 76
  157.1 10.2 %all-to-all-start.1 = ((bf16[16,2,384]{2,1,0:T(2,128)(2,1)}), bf16[16,2,384]{2,1,0:T(2,128)(2,1)S(1)}, u32[]{:S(2)}, u32[]{:S(2)}) async-start(bf16[16,2,384]{2,1,0:T(2,128)(2,1)} %reshape.691), calls=%async_computation.1 | async-start | bytes 49152 | tf_op jit(solution)/shard_map/all_to_all | solution.py:49
  162.3 14.8 %collective-permute-start.2 = (f32[16,1,144]{0,2,1:T(8,128)}, f32[16,1,144]{0,2,1:T(8,128)}, u32[]{:S(2)}, u32[]{:S(2)}) collective-permute-start(f32[16,1,144]{0,2,1:T(8,128)} %get-tuple-element.30), channel_id=1, source_target_pairs={{0,16},{16,32},{32,48},{48,64},{64,80},{80,96},{96,112},{112,128},... | collective-permute-start | bytes 27656 | tf_op jit(solution)/shard_map/ppermute | solution.py:21
  164.9 14.1 %collective-permute-start.3 = (f32[16,1,144]{0,2,1:T(8,128)}, f32[16,1,144]{0,2,1:T(8,128)}, u32[]{:S(2)}, u32[]{:S(2)}) collective-permute-start(f32[16,1,144]{0,2,1:T(8,128)} %get-tuple-element.29), channel_id=1, source_target_pairs={{16,0},{32,16},{48,32},{64,48},{80,64},{96,80},{112,96},{128,112},... | collective-permute-start | bytes 27656 | tf_op jit(solution)/shard_map/ppermute | solution.py:22
  193.2 137.9 %copy-start.10 = (pred[2,144]{1,0:T(4,128)(4,1)S(1)}, pred[2,144]{1,0:T(4,128)(4,1)}, u32[]{:S(2)}) copy-start(pred[2,144]{1,0:T(4,128)(4,1)} %copy-done.9) | copy-start | bytes 868
  193.2 145.2 %copy-start.11 = (f32[16,16]{0,1:T(8,128)S(1)}, f32[16,16]{0,1:T(8,128)}, u32[]{:S(2)}) copy-start(f32[16,16]{0,1:T(8,128)} %fusion.117) | copy-start | bytes 3076
  323.8 3.5 copy-start.12
  327.3 96.8 %all-to-all-start.2 = ((bf16[16,2,384]{2,1,0:T(2,128)(2,1)}), bf16[16,2,384]{2,1,0:T(2,128)(2,1)S(1)}, u32[]{:S(2)}, u32[]{:S(2)}) async-start(bf16[16,2,384]{2,1,0:T(2,128)(2,1)} %reshape.693), calls=%async_computation.2 | async-start | bytes 49152 | tf_op jit(solution)/shard_map/all_to_all | solution.py:49
  332.8 102.1 %collective-permute-start.4 = (f32[16,1,144]{0,2,1:T(8,128)}, f32[16,1,144]{0,2,1:T(8,128)}, u32[]{:S(2)}, u32[]{:S(2)}) collective-permute-start(f32[16,1,144]{0,2,1:T(8,128)} %get-tuple-element.28), channel_id=1, source_target_pairs={{0,16},{16,32},{32,48},{48,64},{64,80},{80,96},{96,112},{112,128},... | collective-permute-start | bytes 27656 | tf_op jit(solution)/shard_map/ppermute | solution.py:21
  334.8 103.7 %collective-permute-start.5 = (f32[16,1,144]{0,2,1:T(8,128)}, f32[16,1,144]{0,2,1:T(8,128)}, u32[]{:S(2)}, u32[]{:S(2)}) collective-permute-start(f32[16,1,144]{0,2,1:T(8,128)} %get-tuple-element.27), channel_id=1, source_target_pairs={{16,0},{32,16},{48,32},{64,48},{80,64},{96,80},{112,96},{128,112},... | collective-permute-start | bytes 27656 | tf_op jit(solution)/shard_map/ppermute | solution.py:22
  423.4 20.6 %copy-start.4 = (f32[16,16]{1,0:T(8,128)}, f32[16,16]{1,0:T(8,128)S(1)}, u32[]{:S(2)}) copy-start(f32[16,16]{1,0:T(8,128)S(1)} %fusion.79) | copy-start | bytes 3076
  551.3 12.8 %all-to-all-start.3 = ((bf16[16,2,384]{2,1,0:T(2,128)(2,1)}), bf16[16,2,384]{2,1,0:T(2,128)(2,1)S(1)}, u32[]{:S(2)}, u32[]{:S(2)}) async-start(bf16[16,2,384]{2,1,0:T(2,128)(2,1)} %reshape.695), calls=%async_computation.3 | async-start | bytes 49152 | tf_op jit(solution)/shard_map/all_to_all | solution.py:49
  556.6 18.5 %collective-permute-start.6 = (f32[16,1,144]{0,2,1:T(8,128)}, f32[16,1,144]{0,2,1:T(8,128)}, u32[]{:S(2)}, u32[]{:S(2)}) collective-permute-start(f32[16,1,144]{0,2,1:T(8,128)} %get-tuple-element.26), channel_id=1, source_target_pairs={{0,16},{16,32},{32,48},{48,64},{64,80},{80,96},{96,112},{112,128},... | collective-permute-start | bytes 27656 | tf_op jit(solution)/shard_map/ppermute | solution.py:21
  559.3 19.6 %collective-permute-start.7 = (f32[16,1,144]{0,2,1:T(8,128)}, f32[16,1,144]{0,2,1:T(8,128)}, u32[]{:S(2)}, u32[]{:S(2)}) collective-permute-start(f32[16,1,144]{0,2,1:T(8,128)} %get-tuple-element.25), channel_id=1, source_target_pairs={{16,0},{32,16},{48,32},{64,48},{80,64},{96,80},{112,96},{128,112},... | collective-permute-start | bytes 27656 | tf_op jit(solution)/shard_map/ppermute | solution.py:22
  713.1 0.6 copy-start.5
  728.2 97.4 %all-to-all-start.4 = ((bf16[16,2,384]{2,1,0:T(2,128)(2,1)}), bf16[16,2,384]{2,1,0:T(2,128)(2,1)}, u32[]{:S(2)}, u32[]{:S(2)}) async-start(bf16[16,2,384]{2,1,0:T(2,128)(2,1)} %reshape.697), calls=%async_computation.4 | async-start | bytes 49152 | tf_op jit(solution)/shard_map/all_to_all | solution.py:49
  734.1 103.1 %collective-permute-start.8 = (f32[16,1,144]{0,2,1:T(8,128)}, f32[16,1,144]{0,2,1:T(8,128)}, u32[]{:S(2)}, u32[]{:S(2)}) collective-permute-start(f32[16,1,144]{0,2,1:T(8,128)} %get-tuple-element.24), channel_id=1, source_target_pairs={{0,16},{16,32},{32,48},{48,64},{64,80},{80,96},{96,112},{112,128},... | collective-permute-start | bytes 27656 | tf_op jit(solution)/shard_map/ppermute | solution.py:21
  736.0 104.7 %collective-permute-start.9 = (f32[16,1,144]{0,2,1:T(8,128)}, f32[16,1,144]{0,2,1:T(8,128)}, u32[]{:S(2)}, u32[]{:S(2)}) collective-permute-start(f32[16,1,144]{0,2,1:T(8,128)} %get-tuple-element.23), channel_id=1, source_target_pairs={{16,0},{32,16},{48,32},{64,48},{80,64},{96,80},{112,96},{128,112},... | collective-permute-start | bytes 27656 | tf_op jit(solution)/shard_map/ppermute | solution.py:22
  824.7 0.6 copy-start.6
  846.0 105.8 %copy-start.3 = (f32[16,1152]{1,0:T(8,128)}, f32[16,1152]{1,0:T(8,128)S(1)}, u32[]{:S(2)}) copy-start(f32[16,1152]{1,0:T(8,128)S(1)} %convolution_subtract_fusion) | copy-start | bytes 221188
  956.5 12.1 %all-to-all-start.5 = ((bf16[16,2,384]{2,1,0:T(2,128)(2,1)}), bf16[16,2,384]{2,1,0:T(2,128)(2,1)S(1)}, u32[]{:S(2)}, u32[]{:S(2)}) async-start(bf16[16,2,384]{2,1,0:T(2,128)(2,1)} %reshape.699), calls=%async_computation.5 | async-start | bytes 49152 | tf_op jit(solution)/shard_map/all_to_all | solution.py:49
  961.7 15.2 %collective-permute-start.10 = (f32[16,1,144]{0,2,1:T(8,128)}, f32[16,1,144]{0,2,1:T(8,128)}, u32[]{:S(2)}, u32[]{:S(2)}) collective-permute-start(f32[16,1,144]{0,2,1:T(8,128)} %get-tuple-element.22), channel_id=1, source_target_pairs={{0,16},{16,32},{32,48},{48,64},{64,80},{80,96},{96,112},{112,128},... | collective-permute-start | bytes 27656 | tf_op jit(solution)/shard_map/ppermute | solution.py:21
  964.5 15.8 %collective-permute-start.11 = (f32[16,1,144]{0,2,1:T(8,128)S(1)}, f32[16,1,144]{0,2,1:T(8,128)}, u32[]{:S(2)}, u32[]{:S(2)}) collective-permute-start(f32[16,1,144]{0,2,1:T(8,128)S(1)} %get-tuple-element.21), channel_id=1, source_target_pairs={{16,0},{32,16},{48,32},{64,48},{80,64},{96,80},{112,96},{128,112},... | collective-permute-start | bytes 27656 | tf_op jit(solution)/shard_map/ppermute | solution.py:22
